TPU v7x, 32 devices: a whole 2x2x4 slice. The times are simulated.
32 devices in a mesh: pipe: 4 (over x, core), tensor: 8 (over z, y).
Axes of the slice: x: 2, y: 2, z: 4, core: 2. Of those that a mesh axis runs over, the one named last changes fastest.
Arguments:
- queries: bfloat16 [8, 64, 16384], P('pipe', None, 'tensor'), may hold values from -10 to 10
- stored_keys: bfloat16 [8, 8192, 1024], P('pipe', 'tensor'), may hold values from -5 to 5
- stored_values: bfloat16 [8, 8192, 1024], P('pipe', 'tensor'), may hold values from -6 to 6
- node_keys: bfloat16 [8, 64, 1024], P('pipe'), may hold values from -10 to 10
- node_values: bfloat16 [8, 64, 1024], P('pipe'), may hold values from -6 to 6
- parents: int32 [8, 64], P('pipe'), may hold values from 0 to 62, as said below
- lengths: int32 [8], P('pipe'), may hold values from 4096 to 8192, as said below
Outputs:
- passed: bfloat16 [8, 64, 16384], P('pipe', None, 'tensor')
Inputs may be any that keep to these rules, and one draw needn't show every extreme that they name: `parents`: node 0 is the root and its entry is 0; the parent of every other node has a lower index, one to four below it or 0; the last node's parent is the node before it. `lengths`: in every draw some request has exactly 8192 live positions and some exactly 4096.
All inputs are finite; a program needn't handle non-finite values.
Results may differ from a plain program's by a relative error of at most 0.01045.
Values may be sent and summed in bfloat16 or wider, within the bound.
A program may use at most 128 MiB of HBM per device.

v0:
```python
import jax
import jax.numpy as jnp
from jax import lax
from jax.sharding import PartitionSpec as P

QUERY_HEADS = 128
KEY_VALUE_HEADS = 8
HEAD_SIZE = 128


MASKED_SCORE = -1e30


def shifted(x, axis, by):
    length = lax.axis_size(axis)
    return lax.ppermute(x, axis, [(i, (i + by) % length) for i in range(length)])


def ancestry(parents):
    tree_node_count = parents.shape[-1]
    node_index = jnp.arange(tree_node_count, dtype=jnp.int32)
    reached = (parents[..., :, None] == node_index).astype(jnp.float32)
    reached = jnp.maximum(reached, jnp.eye(tree_node_count, dtype=jnp.float32))
    for squaring in range(tree_node_count.bit_length()):
        product = jnp.einsum(
            "...ij,...jk->...ik", reached, reached, precision=lax.Precision.HIGHEST
        )
        reached = (product > 0.5).astype(jnp.float32)
    return reached > 0.5


def block_partial(query_row_slice, key_row_slice, value_row_slice, active_mask):
    scale = query_row_slice.shape[-1] ** (-0.5)
    scores = (
        jnp.einsum("id,jd->ij", query_row_slice, key_row_slice, preferred_element_type=jnp.float32)
        * scale
    )
    masked = jnp.where(active_mask[None, :], scores, MASKED_SCORE)
    row_max = jnp.max(masked, axis=1)
    exponent = jnp.where(active_mask[None, :], jnp.exp(masked - row_max[:, None]), 0.0)
    row_sum = jnp.sum(exponent, axis=1)
    numerator = jnp.dot(
        exponent.astype(jnp.bfloat16), value_row_slice, preferred_element_type=jnp.float32
    )
    output = (numerator / jnp.maximum(row_sum, 1.0)[:, None]).astype(jnp.bfloat16)
    return (row_max, row_sum, output)


def tree_partial_all(complete_output, node_keys, node_values, allowed):
    request_list, tree_node_count = (complete_output.shape[0], complete_output.shape[1])
    query_group_size = QUERY_HEADS // KEY_VALUE_HEADS
    query_row_slice = complete_output.reshape(
        request_list, tree_node_count, KEY_VALUE_HEADS, query_group_size, HEAD_SIZE
    )
    key_row_slice = node_keys.reshape(request_list, tree_node_count, KEY_VALUE_HEADS, HEAD_SIZE)
    value_row_slice = node_values.reshape(request_list, tree_node_count, KEY_VALUE_HEADS, HEAD_SIZE)
    scores = jnp.einsum(
        "rnkgd,rjkd->rnkgj", query_row_slice, key_row_slice, preferred_element_type=jnp.float32
    ) * HEAD_SIZE ** (-0.5)
    keep_mask = allowed[:, :, None, None, :]
    masked = jnp.where(keep_mask, scores, MASKED_SCORE)
    row_max = jnp.max(masked, axis=-1)
    exponent = jnp.where(keep_mask, jnp.exp(masked - row_max[..., None]), 0.0)
    row_sum = jnp.sum(exponent, axis=-1)
    numerator = jnp.einsum(
        "rnkgj,rjkd->rnkgd",
        exponent.astype(jnp.bfloat16),
        value_row_slice,
        preferred_element_type=jnp.float32,
    )
    output = numerator / row_sum[..., None]
    return (
        row_max.reshape(request_list, tree_node_count, QUERY_HEADS),
        row_sum.reshape(request_list, tree_node_count, QUERY_HEADS),
        output.reshape(request_list, tree_node_count, QUERY_HEADS, HEAD_SIZE),
    )


def per_device(queries, stored_keys, stored_values, node_keys, node_values, parents, lengths):
    tensor_count = lax.axis_size("tensor")
    tensor_rank = lax.axis_index("tensor")
    complete_output = lax.all_gather(queries, "tensor", axis=2, tiled=True)
    request_list, tree_node_count = (complete_output.shape[0], complete_output.shape[1])
    cache_extent = stored_keys.shape[1]
    query_group_size = QUERY_HEADS // KEY_VALUE_HEADS
    local_heads = QUERY_HEADS // tensor_count
    position = tensor_rank * cache_extent + jnp.arange(cache_extent, dtype=jnp.int32)
    active_mask = position[None, :] < lengths[:, None]
    query_block_list = complete_output.reshape(
        request_list, tree_node_count, KEY_VALUE_HEADS, query_group_size, HEAD_SIZE
    ).transpose(0, 2, 1, 3, 4)
    query_block_list = query_block_list.reshape(
        request_list * KEY_VALUE_HEADS, tree_node_count * query_group_size, HEAD_SIZE
    )
    key_block_list = (
        stored_keys.reshape(request_list, cache_extent, KEY_VALUE_HEADS, HEAD_SIZE)
        .transpose(0, 2, 1, 3)
        .reshape(request_list * KEY_VALUE_HEADS, cache_extent, HEAD_SIZE)
    )
    value_block_list = (
        stored_values.reshape(request_list, cache_extent, KEY_VALUE_HEADS, HEAD_SIZE)
        .transpose(0, 2, 1, 3)
        .reshape(request_list * KEY_VALUE_HEADS, cache_extent, HEAD_SIZE)
    )
    active_blocks = jnp.repeat(active_mask, KEY_VALUE_HEADS, axis=0)
    block_running_max, block_exp_sum, block_result_rows = lax.map(
        lambda operands: block_partial(*operands),
        (query_block_list, key_block_list, value_block_list, active_blocks),
    )
    block_running_max = (
        block_running_max.reshape(request_list, KEY_VALUE_HEADS, tree_node_count, query_group_size)
        .transpose(0, 2, 1, 3)
        .reshape(request_list, tree_node_count, QUERY_HEADS)
    )
    block_exp_sum = (
        block_exp_sum.reshape(request_list, KEY_VALUE_HEADS, tree_node_count, query_group_size)
        .transpose(0, 2, 1, 3)
        .reshape(request_list, tree_node_count, QUERY_HEADS)
    )
    block_result_rows = (
        block_result_rows.reshape(
            request_list, KEY_VALUE_HEADS, tree_node_count, query_group_size, HEAD_SIZE
        )
        .transpose(0, 2, 1, 3, 4)
        .reshape(request_list, tree_node_count, QUERY_HEADS * HEAD_SIZE)
    )
    allowed = ancestry(parents)
    tree_max, tree_sum, tree_out = tree_partial_all(
        complete_output, node_keys, node_values, allowed
    )
    first_head = tensor_rank * local_heads
    own_tree_out = lax.dynamic_slice_in_dim(tree_out, first_head, local_heads, 2)
    every_max, every_sum = (
        lax.all_gather(block_running_max[None], "tensor", axis=0, tiled=True),
        lax.all_gather(block_exp_sum[None], "tensor", axis=0, tiled=True),
    )
    row_best = jnp.maximum(tree_max, jnp.max(every_max, axis=0))
    tree_weight = tree_sum * jnp.exp(tree_max - row_best)
    denominator = tree_weight + jnp.sum(every_sum * jnp.exp(every_max - row_best[None]), axis=0)
    fraction = block_exp_sum * jnp.exp(block_running_max - row_best) / denominator
    weighted = (
        block_result_rows.reshape(request_list, tree_node_count, QUERY_HEADS, HEAD_SIZE).astype(
            jnp.float32
        )
        * fraction[..., None]
    )
    summed = lax.psum_scatter(
        weighted.reshape(request_list, tree_node_count, QUERY_HEADS * HEAD_SIZE).astype(
            jnp.bfloat16
        ),
        "tensor",
        scatter_dimension=2,
        tiled=True,
    ).astype(jnp.float32)
    tree_fraction = lax.dynamic_slice_in_dim(tree_weight / denominator, first_head, local_heads, 2)
    tree_term = (tree_fraction[..., None] * own_tree_out).reshape(
        request_list, tree_node_count, local_heads * HEAD_SIZE
    )
    attended = (summed + tree_term).astype(jnp.bfloat16)
    return shifted(attended, "pipe", 1)


def solution(mesh):
    placed = (
        P("pipe", None, "tensor"),
        P("pipe", "tensor", None),
        P("pipe", "tensor", None),
        P("pipe", None, None),
        P("pipe", None, None),
        P("pipe", None),
        P("pipe"),
    )
    return jax.shard_map(
        per_device, mesh=mesh, in_specs=placed, out_specs=P("pipe", None, "tensor"), check_vma=False
    )
```

profile of v0, /device:TPU:0, one launch (start us, length us, event | category | flops | bytes accessed | tf_op | source)
XLA Modules:
  0.0 417.4 jit_solution(76866023421619704)
XLA Ops:
  11.3 5.3 %copy_bitcast_fusion.2 = bf16[2,1024,8,128]{3,1,2,0:T(8,128)(2,1)} fusion(bf16[2,1024,1024]{2,1,0:T(8,128)(2,1)} %param.10), kind=kLoop, calls=%fused_computation.34 | loop fusion | bytes 8388608 | tf_op jit(solution)/shard_map/reshape | solution.py:96
  19.7 65.9 %all-gather.2.cloned.1.call-done = bf16[2,64,16384]{2,1,0:T(8,128)(2,1)} async-done(((bf16[2,64,2048]{2,1,0:T(8,128)(2,1)}), bf16[2,64,16384]{2,1,0:T(8,128)(2,1)}) %all-gather.2.cloned.1.call-update) | async-done | bytes 4194320 | tf_op jit(solution)/shard_map/all_gather | solution.py:82
  85.7 3.4 copy.106
  89.1 3.2 copy.76
  92.3 99.4 %while.14 = (s32[]{:T(128)}, f32[16,1024]{1,0:T(8,128)S(1)}, f32[16,1024]{1,0:T(8,128)S(1)}, bf16[16,1024,128]{2,1,0:T(8,128)(2,1)}, pred[16,1024]{1,0:T(8,128)(...) while((s32[]{:T(128)}, f32[16,1024]{1,0:T(8,128)S(1)}, ...), condition=%wide.region_3.4_spmd, body=%wide.region_0.3_spmd.sunk | while | flops 550763520 | bytes 13683825 | solution.py:106
  95.2 3.1 fusion.103
  101.4 3.1 fusion.103
  107.6 3.1 fusion.103
  113.9 3.1 fusion.103
  120.1 3.1 fusion.103
  132.5 3.1 fusion.103
  138.7 3.1 fusion.103
  144.9 3.1 fusion.103
  151.1 3.1 fusion.103
  157.4 3.1 fusion.103
  169.8 3.1 fusion.103
  176.0 3.1 fusion.103
  182.2 3.1 fusion.103
  188.4 3.1 fusion.103
  192.2 31.4 %all_gather.10 = f32[8,2,64,128]{3,2,1,0:T(8,128)S(1)} all-gather(f32[1,2,64,128]{3,2,1,0:T(8,128)S(1)} %copy.86), channel_id=1, replica_groups=mesh['pipe'=4,'tensor'=8] {'tensor'}, dimensions={0}, use_global_device_ids=true | all-gather | bytes 589824 | tf_op jit(solution)/shard_map/all_gather | solution.py:134
  223.7 11.5 %fusion.30 = (f32[2,64,8,16]{1,3,2,0:T(8,128)S(1)}, f32[2,8,64,64,16]{3,2,4,1,0:T(8,128)}) fusion(pred[2,64,64]{1,2,0:T(8,128)(4,1)S(1)} %copy.82, bf16[2,64,8,16,128]{4,3,2,1,0:T(8,128)(2,1)} %bitcast.117, bf16[2,64,8,128,1]{3,2,1,0,4:T(8,128)(2,1)S(1)} %bitcast_bitcast_fusion.1), kind=kOutput, calls=%fused_computation.30 | convolution fusion | flops 271564800 | bytes 8724480 | tf_op jit(solution)/shard_map/rnkgd,rjkd->rnkgj/dot_general | solution.py:57
  235.8 31.7 %all_gather.11 = f32[8,2,64,128]{3,2,1,0:T(8,128)S(1)} all-gather(f32[1,2,64,128]{3,2,1,0:T(8,128)S(1)} %copy.93), channel_id=1, replica_groups=mesh['pipe'=4,'tensor'=8] {'tensor'}, dimensions={0}, use_global_device_ids=true | all-gather | bytes 589824 | tf_op jit(solution)/shard_map/all_gather | solution.py:135
  267.5 6.7 %fusion.31 = (bf16[2,64,8,16,64]{1,4,3,2,0:T(8,128)(2,1)}, f32[2,64,8,16]{1,3,2,0:T(8,128)S(1)}) fusion(f32[2,8,64,64,16]{3,2,4,1,0:T(8,128)} %get-tuple-element.76, f32[2,64,8,16]{1,3,2,0:T(8,128)S(1)} %get-tuple-element.75, pred[2,64,64]{1,2,0:T(8,128)(4,1)S(1)} %copy.82), kind=kLoop, calls=%fused_computation.31 | loop fusion | flops 6275072 | bytes 6430720 | tf_op jit(solution)/shard_map/convert_element_type | solution.py:67
  274.6 4.6 %mul.61 = f32[2,64,128,128]{3,2,1,0:T(8,128)} broadcast(f32[2,64,128]{2,1,0:T(8,128)S(1)} %get-tuple-element.68), dimensions={0,1,2} | broadcast | bytes 8454144 | tf_op jit(solution)/shard_map/mul | solution.py:142
  279.2 9.4 %mul.62 = f32[2,64,16384]{2,1,0:T(8,128)} reshape(f32[2,64,128,128]{3,2,1,0:T(8,128)} %mul.61) | data formatting | bytes 16777216 | tf_op jit(solution)/shard_map/mul | solution.py:142
  288.6 6.6 %copy_bitcast_fusion = f32[2,64,8,16,128]{4,3,2,1,0:T(8,128)} fusion(bf16[2,8,64,16,128]{4,3,2,1,0:T(8,128)(2,1)} %bitcast.121), kind=kLoop, calls=%fused_computation.27 | loop fusion | flops 2097152 | bytes 12582912 | tf_op jit(solution)/shard_map/convert_element_type | solution.py:142
  295.1 9.4 %reshape.138 = f32[2,64,16384]{2,1,0:T(8,128)} reshape(f32[2,64,8,16,128]{4,3,2,1,0:T(8,128)} %copy_bitcast_fusion) | data formatting | bytes 16777216 | tf_op jit(solution)/shard_map/convert_element_type | solution.py:142
  304.5 8.5 %multiply_convert_fusion = bf16[2,64,16384]{2,1,0:T(8,128)(2,1)} fusion(f32[2,64,16384]{2,1,0:T(8,128)} %reshape.138, f32[2,64,16384]{2,1,0:T(8,128)} %mul.62), kind=kLoop, calls=%fused_computation.28 | loop fusion | flops 4194304 | bytes 20971520 | tf_op jit(solution)/shard_map/convert_element_type | solution.py:148
  314.3 7.1 %copy.94 = bf16[2,64,8,16,64]{4,3,1,2,0:T(8,128)(2,1)} copy(bf16[2,64,8,16,64]{1,4,3,2,0:T(8,128)(2,1)} %get-tuple-element.73) | data formatting | bytes 4194304 | tf_op jit(solution)/shard_map/convert_element_type | solution.py:67
  321.4 4.6 %bitcast_divide_fusion = f32[2,64,8,16,128]{4,3,1,2,0:T(8,128)S(1)} fusion(f32[2,64,8,16]{3,1,2,0:T(8,128)S(1)} %copy.96, bf16[2,64,8,16,64]{4,3,1,2,0:T(8,128)(2,1)} %copy.94, bf16[2,64,8,128,1]{3,2,1,0,4:T(8,128)(2,1)S(1)} %bitcast_bitcast_fusion), kind=kOutput, calls=%fused_computation.25 | convolution fusion | flops 270532608 | bytes 10813440 | tf_op jit(solution)/shard_map/rnkgj,rjkd->rnkgd/dot_general | solution.py:65
  327.9 72.0 %reduce-scatter.2.cloned.1.call-done = bf16[2,64,2048]{2,1,0:T(8,128)(2,1)} async-done(((bf16[2,64,16384]{2,1,0:T(8,128)(2,1)}), bf16[2,64,2048]{2,1,0:T(8,128)(2,1)}) %reduce-scatter.2.cloned.1.call-update) | async-done | bytes 524304 | tf_op jit(solution)/shard_map/reduce_scatter | solution.py:147
  401.1 8.6 %collective-permute-done = bf16[2,64,2048]{2,1,0:T(8,128)(2,1)S(1)} collective-permute-done((bf16[2,64,2048]{2,1,0:T(8,128)(2,1)S(1)}, bf16[2,64,2048]{2,1,0:T(8,128)(2,1)S(1)}, u32[]{:S(2)}, u32[]{:S(2)}) %collective-permute-start) | collective-permute-done | bytes 524320 | tf_op jit(solution)/shard_map/ppermute | solution.py:16
  (156 shorter events, 69.1 us)
Async XLA Ops:
  6.5 79.1 %all-gather.2.cloned.1.call-start = ((), (), s32[]{:S(2)}) async-start(), calls=%async_computation.1 | async-start | bytes 4718592 | tf_op jit(solution)/shard_map/all_gather | solution.py:82
  7.3 392.7 %reduce-scatter.2.cloned.1.call-start = ((), (), s32[]{:S(2)}) async-start(), calls=%async_computation.2 | async-start | bytes 4718592 | tf_op jit(solution)/shard_map/reduce_scatter | solution.py:147
  11.3 5.4 %copy-start.1 = (bf16[2,1024,1024]{2,1,0:T(8,128)(2,1)S(1)}, bf16[2,1024,1024]{2,1,0:T(8,128)(2,1)}, u32[]{:S(2)}) copy-start(bf16[2,1024,1024]{2,1,0:T(8,128)(2,1)} %param.11) | copy-start | bytes 12582916
  89.1 3.2 copy-start
  313.1 0.9 copy-start.2
  401.1 8.7 %collective-permute-start = (bf16[2,64,2048]{2,1,0:T(8,128)(2,1)S(1)}, bf16[2,64,2048]{2,1,0:T(8,128)(2,1)S(1)}, u32[]{:S(2)}, u32[]{:S(2)}) collective-permute-start(bf16[2,64,2048]{2,1,0:T(8,128)(2,1)S(1)} %add_convert_fusion), channel_id=1, source_target_pairs={{0,8},{8,16},{16,24},{24,0},{1,9},{9,17},{17,25},{25,1},{2,10},{10... | collective-permute-start | bytes 1572872 | tf_op jit(solution)/shard_map/ppermute | solution.py:16
Sparse Core Ops, SparseCore 0:
  9.5 76.0 all-gather.1
  313.2 86.6 reduce-scatter.1
where the time goes:
time: 419 us; the launch traced here: 417 us
  waiting for transfers between devices  147 us (35%)
  matrix products  96.1 us (23%)
  blocking collectives  63.1 us (15%)
  local copies, waits for them, and re-layouts  54.6 us (13%)
  other arithmetic  41.5 us (10%)
  between operations  13.7 us (3%)
    reduce_scatter x1, waiting for transfers between devices, per_device(): lax.psum_scatter(weighted.reshape(request_list, tree_node_count, QUERY_HE...  72 us
    all_gather x1, waiting for transfers between devices, per_device(): complete_output = lax.all_gather(queries, 'tensor', axis=2, tiled=True)  65.9 us
    dot_general x16, matrix products, block_partial(): jnp.dot(exponent.astype(jnp.bfloat16), value_row_slice, preferred_element...  49.9 us
    all_gather x1, blocking collectives, per_device(): lax.all_gather(block_exp_sum[None], 'tensor', axis=0, tiled=True)  31.7 us
    all_gather x1, blocking collectives, per_device(): lax.all_gather(block_running_max[None], 'tensor', axis=0, tiled=True)  31.4 us
    dot_general x16, matrix products, block_partial(): jnp.einsum('id,jd->ij', query_row_slice, key_row_slice, preferred_element...  28.2 us
    reduce_sum x16, other arithmetic, block_partial(): row_sum = jnp.sum(exponent, axis=1)  17 us
    mul x2, local copies, waits for them, and re-layouts, per_device(): block_result_rows.reshape(request_list, tree_node_count, QUERY_HEADS, HEA...  14 us
  transfers between devices with their start and end apart: 3, of which 3 were waited for; matrix products, arithmetic and copies ran while one was open for 6% of the time, Pallas kernels for 0%

commit v1 on v0

v1 whole, which is shorter than its diff:
```python
import functools

import jax
import jax.numpy as jnp
from jax import lax
from jax.experimental import pallas as pl
from jax.experimental.pallas import tpu as pltpu
from jax.sharding import PartitionSpec as P

QUERY_HEADS = 128
KEY_VALUE_HEADS = 8
HEAD_SIZE = 128
MASKED_SCORE = -1e30
NT = (((1,), (1,)), ((), ()))
TN = (((0,), (0,)), ((), ()))


def head_rows(block):
    heads = block.shape[1] // HEAD_SIZE
    return jnp.concatenate(
        [block[:, h * HEAD_SIZE : (h + 1) * HEAD_SIZE] for h in range(heads)], axis=0
    )


def block_kernel(first_ref, lengths_ref, q_ref, k_ref, v_ref, o_ref, stat_ref):
    live = lengths_ref[pl.program_id(0)] - first_ref[0]
    keys = k_ref[0]
    values = v_ref[0]
    positions = lax.broadcasted_iota(jnp.int32, (keys.shape[0], 1), 0)
    active = positions < live
    scale = HEAD_SIZE**-0.5
    for part in range(q_ref.shape[0]):
        heads = q_ref.shape[3] // HEAD_SIZE
        for first in range(0, heads, 4):
            rows = head_rows(q_ref[part, 0, :, first * HEAD_SIZE : (first + 4) * HEAD_SIZE])
            scores = lax.dot_general(keys, rows, NT, preferred_element_type=jnp.float32)
            scores = jnp.where(active, scores * scale, MASKED_SCORE)
            top = jnp.max(scores, axis=0, keepdims=True)
            weights = jnp.exp(scores - top)
            total = jnp.sum(weights, axis=0, keepdims=True)
            out = lax.dot_general(
                values, weights.astype(jnp.bfloat16), TN, preferred_element_type=jnp.float32
            )
            columns = slice(first * 64, (first + 4) * 64)
            o_ref[part, 0, :, columns] = (out / total).astype(jnp.bfloat16)
            stat_ref[part, 0, 0:1, columns] = top
            stat_ref[part, 0, 1:2, columns] = total


def block_attention(queries, keys, values, first, lengths):
    ranks, requests, nodes, width = queries.shape
    extent = keys.shape[1]
    share = ranks // KEY_VALUE_HEADS
    rows = width // HEAD_SIZE * nodes
    return pl.pallas_call(
        block_kernel,
        grid=(requests, KEY_VALUE_HEADS),
        in_specs=[
            pl.BlockSpec(memory_space=pltpu.SMEM),
            pl.BlockSpec(memory_space=pltpu.SMEM),
            pl.BlockSpec((share, 1, nodes, width), lambda r, g: (g, r, 0, 0)),
            pl.BlockSpec((1, extent, HEAD_SIZE), lambda r, g: (r, 0, g)),
            pl.BlockSpec((1, extent, HEAD_SIZE), lambda r, g: (r, 0, g)),
        ],
        out_specs=[
            pl.BlockSpec((share, 1, HEAD_SIZE, rows), lambda r, g: (g, r, 0, 0)),
            pl.BlockSpec((share, 1, 2, rows), lambda r, g: (g, r, 0, 0)),
        ],
        out_shape=[
            jax.ShapeDtypeStruct((ranks, requests, HEAD_SIZE, rows), jnp.bfloat16),
            jax.ShapeDtypeStruct((ranks, requests, 2, rows), jnp.float32),
        ],
        compiler_params=pltpu.CompilerParams(vmem_limit_bytes=40 << 20),
    )(first, lengths, queries, keys, values)


def tree_part(rows, node_keys, node_values, parents):
    nodes = node_keys.shape[0]
    row = lax.broadcasted_iota(jnp.int32, (nodes, nodes), 0)
    column = lax.broadcasted_iota(jnp.int32, (nodes, nodes), 1)
    reached = ((parents == row) | (row == column)).astype(jnp.bfloat16)
    for squaring in range(nodes.bit_length()):
        product = jnp.dot(reached, reached, preferred_element_type=jnp.float32)
        reached = (product > 0.5).astype(jnp.bfloat16)
    width = rows.shape[0]
    node = lax.broadcasted_iota(jnp.int32, (nodes, width), 0)
    owner = lax.rem(lax.broadcasted_iota(jnp.int32, (nodes, width), 1), nodes)
    spread = (node == owner).astype(jnp.bfloat16)
    allowed = jnp.dot(reached, spread, preferred_element_type=jnp.float32) > 0.5
    scores = lax.dot_general(node_keys, rows, NT, preferred_element_type=jnp.float32)
    scores = jnp.where(allowed, scores * HEAD_SIZE**-0.5, MASKED_SCORE)
    top = jnp.max(scores, axis=0, keepdims=True)
    weights = jnp.where(allowed, jnp.exp(scores - top), 0.0)
    total = jnp.sum(weights, axis=0, keepdims=True)
    out = lax.dot_general(
        node_values, weights.astype(jnp.bfloat16), TN, preferred_element_type=jnp.float32
    )
    return top, total, out / total


def join_kernel(q_ref, nk_ref, nv_ref, parents_ref, summed_ref, stat_ref, out_ref):
    nodes = q_ref.shape[1]
    top, total, tree = tree_part(head_rows(q_ref[0]), nk_ref[0], nv_ref[0], parents_ref[0])
    block_top, block_total = stat_ref[0, 0:1], stat_ref[0, 1:2]
    best = jnp.maximum(top, block_top)
    a = total * jnp.exp(top - best)
    c = block_total * jnp.exp(block_top - best)
    joined = (a * tree + c * summed_ref[0].astype(jnp.float32)) / (a + c)
    joined = joined.T.astype(out_ref.dtype)
    for h in range(q_ref.shape[2] // HEAD_SIZE):
        out_ref[0, :, h * HEAD_SIZE : (h + 1) * HEAD_SIZE] = joined[h * nodes : (h + 1) * nodes]


def join(queries, node_keys, node_values, parents, summed, stats):
    def one(x):
        return pl.BlockSpec((1,) + x.shape[1:], lambda r: (r,) + (0,) * (x.ndim - 1))

    operands = (queries, node_keys, node_values, parents[:, None, :], summed, stats)
    return pl.pallas_call(
        join_kernel,
        grid=(queries.shape[0],),
        in_specs=[one(x) for x in operands],
        out_specs=one(queries),
        out_shape=jax.ShapeDtypeStruct(queries.shape, jnp.bfloat16),
        compiler_params=pltpu.CompilerParams(vmem_limit_bytes=32 << 20),
    )(*operands)


def per_device(queries, stored_keys, stored_values, node_keys, node_values, parents, lengths):
    ranks = lax.axis_size("tensor")
    rank = lax.axis_index("tensor")
    extent = stored_keys.shape[1]
    every = lax.all_gather(queries, "tensor", axis=0, tiled=False)
    first = (rank * extent).astype(jnp.int32)[None]
    outs, stats = block_attention(every, stored_keys, stored_values, first, lengths)
    every_stat = lax.all_gather(stats, "tensor", axis=0, tiled=False)
    best = jnp.max(every_stat[:, :, :, 0], axis=0)
    total = jnp.sum(every_stat[:, :, :, 1] * jnp.exp(every_stat[:, :, :, 0] - best), axis=0)
    fraction = stats[:, :, 1] * jnp.exp(stats[:, :, 0] - best) / total
    weighted = (outs.astype(jnp.float32) * fraction[:, :, None, :]).astype(jnp.bfloat16)
    summed = lax.psum_scatter(weighted, "tensor", scatter_dimension=0, tiled=False)
    own_stats = lax.dynamic_index_in_dim(jnp.stack([best, total], axis=2), rank, 0, keepdims=False)
    group = rank * KEY_VALUE_HEADS // ranks
    own_keys = lax.dynamic_slice_in_dim(node_keys, group * HEAD_SIZE, HEAD_SIZE, 2)
    own_values = lax.dynamic_slice_in_dim(node_values, group * HEAD_SIZE, HEAD_SIZE, 2)
    attended = join(queries, own_keys, own_values, parents, summed, own_stats)
    length = lax.axis_size("pipe")
    return lax.ppermute(attended, "pipe", [(i, (i + 1) % length) for i in range(length)])


def solution(mesh):
    placed = (
        P("pipe", None, "tensor"),
        P("pipe", "tensor", None),
        P("pipe", "tensor", None),
        P("pipe", None, None),
        P("pipe", None, None),
        P("pipe", None),
        P("pipe"),
    )
    return jax.shard_map(
        per_device, mesh=mesh, in_specs=placed, out_specs=P("pipe", None, "tensor"), check_vma=False
    )
```

time: 419 us -> 300 us (0.72)
  matrix products: 96.1 us -> 0 us
  waiting for transfers between devices: 147 us -> 212 us
  blocking collectives: 63.1 us -> 0 us
  Pallas kernels: 0 us -> 54.2 us
  local copies, waits for them, and re-layouts: 54.6 us -> 9.79 us
  other arithmetic: 41.5 us -> 9.96 us
    dot_general x41 -> x0, matrix products: 96.1 us -> none  [the longest x16 49.9 us: block_partial(): jnp.dot(exponent.astype(jnp.bfloat16), value_row_slice, preferred_element...]
    all_gather x2 -> x0, blocking collectives: 63.1 us -> none  [the longest x1 31.7 us: per_device(): lax.all_gather(block_exp_sum[None], 'tensor', axis=0, tiled=True)]
    pallas_call x0 -> x2, Pallas kernels: none -> 54.2 us  [the longest x1 51.3 us: block_attention(): pl.pallas_call(block_kernel, grid=(requests, KEY_VALUE_HEADS), in_specs=[...]
    all_gather x1 -> x2, waiting for transfers between devices: 65.9 us -> 117 us  [the longest x1 78.3 us: per_device(): every = lax.all_gather(queries, 'tensor', axis=0, tiled=False)]
    convert_element_type x5 -> x1, other arithmetic: 22.9 us -> 5.43 us  [per_device(): (outs.astype(jnp.float32) * fraction[:, :, None, :]).astype(jnp.bfloat16)]
    reduce_sum x17 -> x1, other arithmetic: 17.1 us -> 0.55 us  [per_device(): jnp.sum(every_stat[:, :, :, 1] * jnp.exp(every_stat[:, :, :, 0] - best),...]
    convert_element_type x2 -> x0, local copies, waits for them, and re-layouts: 16.5 us -> none  [the longest x1 9.39 us: per_device(): block_result_rows.reshape(request_list, tree_node_count, QUERY_HEADS, HEA...]
    mul x2 -> x0, local copies, waits for them, and re-layouts: 14 us -> none  [per_device(): block_result_rows.reshape(request_list, tree_node_count, QUERY_HEADS, HEA...]
  transfers between devices with their start and end apart: 3 -> 4, of which waited for: 3 -> 4; matrix products, arithmetic and copies ran while one was open for 6% -> 0% of each run, Pallas kernels for 0% -> 0%
where the time goes in v1:
time: 300 us; the launch traced here: 299 us
  waiting for transfers between devices  212 us (71%)
  Pallas kernels  54.2 us (18%)
  between operations  13.2 us (4%)
  other arithmetic  9.96 us (3%)
  local copies, waits for them, and re-layouts  9.79 us (3%)
    reduce_scatter x1, waiting for transfers between devices, per_device(): lax.psum_scatter(weighted, 'tensor', scatter_dimension=0, tiled=False)  85.8 us
    all_gather x1, waiting for transfers between devices, per_device(): every = lax.all_gather(queries, 'tensor', axis=0, tiled=False)  78.3 us
    pallas_call x1, Pallas kernels, block_attention(): pl.pallas_call(block_kernel, grid=(requests, KEY_VALUE_HEADS), in_specs=[...  51.3 us
    all_gather x1, waiting for transfers between devices, per_device(): every_stat = lax.all_gather(stats, 'tensor', axis=0, tiled=False)  38.5 us
    unnamed x16, local copies, waits for them, and re-layouts  8.86 us
    ppermute x1, waiting for transfers between devices, per_device(): lax.ppermute(attended, 'pipe', [(i, (i + 1) % length) for i in range(leng...  8.59 us
  transfers between devices with their start and end apart: 4, of which 4 were waited for; matrix products, arithmetic and copies ran while one was open for 0% of the time, Pallas kernels for 0%

profile of v1, /device:TPU:0, one launch (start us, length us, event | category | flops | bytes accessed | tf_op | source)
XLA Modules:
  0.0 299.3 jit_solution(5511301353063292939)
XLA Ops:
  6.5 0.0 all-gather.5.cloned.1.call-start
  6.5 0.7 all-gather.5.cloned.1.call-update
  7.3 0.0 all-gather.7.cloned.1.call-start
  7.3 78.3 %all-gather.5.cloned.1.call-done = bf16[16,64,2048]{2,1,0:T(8,128)(2,1)} async-done(((bf16[2,64,2048]{2,1,0:T(8,128)(2,1)}), bf16[16,64,2048]{2,1,0:T(8,128)(2,1)}) %all-gather.5.cloned.1.call-update) | async-done | bytes 4194320 | tf_op jit(solution)/shard_map/all_gather | solution.py:133
  85.6 0.0 copy-start
  85.6 2.2 copy-done
  87.8 0.0 copy-start.1
  87.8 2.2 copy-done.1
  90.0 0.0 copy-start.6
  90.0 0.7 copy-done.6
  90.6 51.3 %shard_map.73 = (bf16[8,2,128,1024]{3,2,1,0:T(8,128)(2,1)S(1)}, f32[8,2,2,1024]{3,2,1,0:T(2,128)}) custom-call(s32[1]{0:T(128)} %bitcast.2.first_ref, s32[2]{0:T(128)S(1)} %copy-done.6, bf16[8,2,64,2048]{3,2,1,0:T(8,128)(2,1)S(1)} %bitcast.26, bf16[2,1024,1024]{2,1,0:T(8,128)(2,1)S(1)} %copy-done, bf16[2,1024,1024]{2,1,0:T(8,128)(2,1)} %v_ref.1), custom_call_target="tpu_custom_call" | custom-call | tf_op jit(solution)/shard_map/pallas_call | solution.py:55
  141.9 0.0 copy-start.2
  141.9 2.0 copy-done.2
  143.9 0.0 all-gather.7.cloned.1.call-update
  143.9 0.0 reduce-scatter.2.cloned.1.call-start
  144.0 38.5 %all-gather.7.cloned.1.call-done = f32[64,2,2,1024]{3,2,1,0:T(2,128)} async-done(((f32[8,2,2,1024]{3,2,1,0:T(2,128)}), f32[64,2,2,1024]{3,2,1,0:T(2,128)}) %all-gather.7.cloned.1.call-update) | async-done | bytes 1048592 | tf_op jit(solution)/shard_map/all_gather | solution.py:136
  182.5 2.8 slice_reduce_fusion
  185.3 0.5 fusion.3
  185.8 1.2 multiply_divide_fusion
  187.0 5.4 %multiply_convert_fusion = bf16[8,2,128,1024]{3,2,1,0:T(8,128)(2,1)} fusion(bf16[8,2,128,1024]{3,2,1,0:T(8,128)(2,1)} %copy-done.2, f32[8,2,1024]{2,1,0:T(2,128)S(1)} %bitcast.30), kind=kLoop, calls=%fused_computation | loop fusion | flops 6291456 | bytes 8454144 | tf_op jit(solution)/shard_map/convert_element_type | solution.py:140
  192.5 0.0 copy-start.3
  192.5 0.0 copy-start.5
  192.5 0.0 reduce-scatter.2.cloned.1.call-update
  192.5 0.8 constant_dynamic-slice_fusion
  193.5 85.8 %reduce-scatter.2.cloned.1.call-done = bf16[1,2,128,1024]{3,2,1,0:T(8,128)(2,1)} async-done(((bf16[8,2,128,1024]{3,2,1,0:T(8,128)(2,1)}), bf16[1,2,128,1024]{3,2,1,0:T(8,128)(2,1)}) %reduce-scatter.2.cloned.1.call-update) | async-done | bytes 524304 | tf_op jit(solution)/shard_map/reduce_scatter | solution.py:141
  279.3 0.0 copy-done.3
  279.3 0.0 copy-done.5
  279.3 1.0 copy-done.4
  280.4 3.0 shard_map.74
  283.3 0.1 collective-permute-start
  283.4 8.6 %collective-permute-done = bf16[2,64,2048]{2,1,0:T(8,128)(2,1)S(1)} collective-permute-done((bf16[2,64,2048]{2,1,0:T(8,128)(2,1)S(1)}, bf16[2,64,2048]{2,1,0:T(8,128)(2,1)S(1)}, u32[]{:S(2)}, u32[]{:S(2)}) %collective-permute-start) | collective-permute-done | bytes 524320 | tf_op jit(solution)/shard_map/ppermute | solution.py:148
  292.0 0.8 copy.31
  (5 shorter events, 0.2 us)
Async XLA Ops:
  6.5 79.1 %all-gather.5.cloned.1.call-start = ((), (), s32[]{:S(2)}) async-start(), calls=%async_computation.2 | async-start | bytes 4718592 | tf_op jit(solution)/shard_map/all_gather | solution.py:133
  7.3 175.2 %all-gather.7.cloned.1.call-start = ((), (), s32[]{:S(2)}) async-start(), calls=%async_computation.3 | async-start | bytes 1179648 | tf_op jit(solution)/shard_map/all_gather | solution.py:136
  85.6 2.2 copy-start
  87.8 2.2 copy-start.1
  90.0 0.7 copy-start.6
  141.9 2.0 copy-start.2
  143.9 135.4 %reduce-scatter.2.cloned.1.call-start = ((), (), s32[]{:S(2)}) async-start(), calls=%async_computation.1 | async-start | bytes 4718592 | tf_op jit(solution)/shard_map/reduce_scatter | solution.py:141
  192.5 86.9 %copy-start.3 = (bf16[2,64,2048]{2,1,0:T(8,128)(2,1)S(1)}, bf16[2,64,2048]{2,1,0:T(8,128)(2,1)}, u32[]{:S(2)}) copy-start(bf16[2,64,2048]{2,1,0:T(8,128)(2,1)} %q_ref.1) | copy-start | bytes 1572868
  192.5 86.9 %copy-start.5 = (s32[2,64]{1,0:T(2,128)S(1)}, s32[2,64]{1,0:T(2,128)}, u32[]{:S(2)}) copy-start(s32[2,64]{1,0:T(2,128)} %param.12) | copy-start | bytes 1540
  279.3 1.0 copy-start.4
  283.3 8.7 %collective-permute-start = (bf16[2,64,2048]{2,1,0:T(8,128)(2,1)S(1)}, bf16[2,64,2048]{2,1,0:T(8,128)(2,1)S(1)}, u32[]{:S(2)}, u32[]{:S(2)}) collective-permute-start(bf16[2,64,2048]{2,1,0:T(8,128)(2,1)S(1)} %shard_map.74), channel_id=1, source_target_pairs={{0,8},{8,16},{16,24},{24,0},{1,9},{9,17},{17,25},{25,1},{2,10},{10... | collective-permute-start | bytes 1572872 | tf_op jit(solution)/shard_map/ppermute | solution.py:148
Sparse Core Ops, SparseCore 0:
  9.5 76.0 all-gather.4
  144.0 38.3 all-gather.6
  192.6 86.6 reduce-scatter.1

commit v2 on v1

--- a/solution.py
+++ b/solution.py
@@ -11,6 +11,7 @@
 KEY_VALUE_HEADS = 8
 HEAD_SIZE = 128
 MASKED_SCORE = -1e30
+LOG2_E = 1.4426950408889634
 NT = (((1,), (1,)), ((), ()))
 TN = (((0,), (0,)), ((), ()))
 
@@ -34,16 +35,16 @@
         for first in range(0, heads, 4):
             rows = head_rows(q_ref[part, 0, :, first * HEAD_SIZE : (first + 4) * HEAD_SIZE])
             scores = lax.dot_general(keys, rows, NT, preferred_element_type=jnp.float32)
-            scores = jnp.where(active, scores * scale, MASKED_SCORE)
+            scores = jnp.where(active, scores, MASKED_SCORE)
             top = jnp.max(scores, axis=0, keepdims=True)
-            weights = jnp.exp(scores - top)
+            weights = jnp.exp2((scores - top) * (scale * LOG2_E))
             total = jnp.sum(weights, axis=0, keepdims=True)
             out = lax.dot_general(
                 values, weights.astype(jnp.bfloat16), TN, preferred_element_type=jnp.float32
             )
             columns = slice(first * 64, (first + 4) * 64)
             o_ref[part, 0, :, columns] = (out / total).astype(jnp.bfloat16)
-            stat_ref[part, 0, 0:1, columns] = top
+            stat_ref[part, 0, 0:1, columns] = top * scale
             stat_ref[part, 0, 1:2, columns] = total
 
 
@@ -98,52 +99,236 @@
     return top, total, out / total
 
 
-def join_kernel(q_ref, nk_ref, nv_ref, parents_ref, summed_ref, stat_ref, out_ref):
-    nodes = q_ref.shape[1]
-    top, total, tree = tree_part(head_rows(q_ref[0]), nk_ref[0], nv_ref[0], parents_ref[0])
-    block_top, block_total = stat_ref[0, 0:1], stat_ref[0, 1:2]
-    best = jnp.maximum(top, block_top)
-    a = total * jnp.exp(top - best)
-    c = block_total * jnp.exp(block_top - best)
-    joined = (a * tree + c * summed_ref[0].astype(jnp.float32)) / (a + c)
-    joined = joined.T.astype(out_ref.dtype)
-    for h in range(q_ref.shape[2] // HEAD_SIZE):
-        out_ref[0, :, h * HEAD_SIZE : (h + 1) * HEAD_SIZE] = joined[h * nodes : (h + 1) * nodes]
-
-
-def join(queries, node_keys, node_values, parents, summed, stats):
-    def one(x):
-        return pl.BlockSpec((1,) + x.shape[1:], lambda r: (r,) + (0,) * (x.ndim - 1))
-
-    operands = (queries, node_keys, node_values, parents[:, None, :], summed, stats)
+def peer(z, y, across):
+    return {"tensor": z * across + y}
+
+
+def remote(source, target, sends, receives, at, device):
+    return pltpu.make_async_remote_copy(
+        src_ref=source,
+        dst_ref=target,
+        send_sem=sends.at[at],
+        recv_sem=receives.at[at],
+        device_id=device,
+        device_id_type=pl.DeviceIdType.MESH,
+    )
+
+
+def greet(deep, across, z, y):
+    barrier = pltpu.get_barrier_semaphore()
+    partners = [peer(lax.rem(z + dz, deep), y, across) for dz in range(1, deep)]
+    partners += [peer(z, lax.rem(y + dy, across), across) for dy in range(1, across)]
+    for partner in partners:
+        pl.semaphore_signal(
+            barrier, inc=1, device_id=partner, device_id_type=pl.DeviceIdType.MESH
+        )
+    pl.semaphore_wait(barrier, len(partners))
+
+
+def gather_kernel(
+    deep, across, q_ref, every_ref, own_sem, z_send, z_receive, y_send, y_receive
+):
+    rank = lax.axis_index("tensor")
+    z, y = rank // across, lax.rem(rank, across)
+    greet(deep, across, z, y)
+    requests = q_ref.shape[0]
+    own = pltpu.make_async_copy(q_ref, every_ref.at[rank], own_sem)
+    own.start()
+    along_z, along_y = [], []
+    for r in range(requests):
+        for dz in range(1, deep):
+            copy = remote(
+                q_ref.at[r],
+                every_ref.at[rank, r],
+                z_send,
+                z_receive,
+                (r, dz - 1),
+                peer(lax.rem(z + dz, deep), y, across),
+            )
+            copy.start()
+            along_z.append(copy)
+        for dy in range(1, across):
+            copy = remote(
+                q_ref.at[r],
+                every_ref.at[rank, r],
+                y_send,
+                y_receive,
+                (r, 0, dy - 1),
+                peer(z, lax.rem(y + dy, across), across),
+            )
+            copy.start()
+            along_y.append(copy)
+    for r in range(requests):
+        for dz in range(1, deep):
+            source = lax.rem(z + deep - dz, deep) * across + y
+            remote(
+                q_ref.at[r], every_ref.at[source, r], z_send, z_receive, (r, dz - 1),
+                peer(lax.rem(z + dz, deep), y, across),
+            ).wait_recv()
+            for dy in range(1, across):
+                copy = remote(
+                    every_ref.at[source, r],
+                    every_ref.at[source, r],
+                    y_send,
+                    y_receive,
+                    (r, dz, dy - 1),
+                    peer(z, lax.rem(y + dy, across), across),
+                )
+                copy.start()
+                along_y.append(copy)
+    for copy in along_z:
+        copy.wait_send()
+    for copy in along_y:
+        copy.wait()
+    own.wait()
+
+
+def gather(queries, ranks):
+    deep = 4
+    across = ranks // deep
+    requests = queries.shape[0]
+    semaphore = pltpu.SemaphoreType.DMA
     return pl.pallas_call(
-        join_kernel,
-        grid=(queries.shape[0],),
-        in_specs=[one(x) for x in operands],
-        out_specs=one(queries),
+        functools.partial(gather_kernel, deep, across),
+        in_specs=[pl.BlockSpec(memory_space=pltpu.VMEM)],
+        out_specs=pl.BlockSpec(memory_space=pltpu.VMEM),
+        out_shape=jax.ShapeDtypeStruct((ranks,) + queries.shape, queries.dtype),
+        scratch_shapes=[
+            semaphore,
+            semaphore((requests, deep - 1)),
+            semaphore((requests, deep - 1)),
+            semaphore((requests, deep, across - 1)),
+            semaphore((requests, deep, across - 1)),
+        ],
+        compiler_params=pltpu.CompilerParams(
+            collective_id=0, has_side_effects=True, vmem_limit_bytes=32 << 20
+        ),
+    )(queries)
+
+
+def combine(parts):
+    best = functools.reduce(jnp.maximum, [top for top, total, mean in parts])
+    shares = [total * jnp.exp(top - best) for top, total, mean in parts]
+    whole = sum(shares[1:], shares[0])
+    mean = sum(
+        (share / whole) * part[2].astype(jnp.float32) for share, part in zip(shares, parts)
+    )
+    return best, whole, mean
+
+
+def join_kernel(
+    deep, across, q_ref, nk_ref, nv_ref, parents_ref, o_ref, stat_ref, out_ref,
+    y_o, y_stat, held_o, held_stat, z_o, z_stat,
+    yo_send, yo_receive, ys_send, ys_receive, zo_send, zo_receive, zs_send, zs_receive,
+):
+    rank = lax.axis_index("tensor")
+    z, y = rank // across, lax.rem(rank, across)
+    greet(deep, across, z, y)
+    requests, nodes, width = q_ref.shape
+    along_y, along_z = [], []
+    for dz in [*range(1, deep), 0]:
+        slots = []
+        for dy in range(1, across):
+            other = lax.rem(y + dy, across)
+            slot = lax.rem(z + dz, deep) * across + other
+            at = (dz, dy - 1)
+            device = peer(z, other, across)
+            pair = (
+                remote(o_ref.at[slot], y_o.at[at], yo_send, yo_receive, at, device),
+                remote(stat_ref.at[slot], y_stat.at[at], ys_send, ys_receive, at, device),
+            )
+            for copy in pair:
+                copy.start()
+            slots.append(pair)
+        along_y.append((dz, slots))
+    for dz, slots in along_y:
+        for pair in slots:
+            for copy in pair:
+                copy.wait_recv()
+        mine = lax.rem(z + dz, deep) * across + y
+        for r in range(requests):
+            parts = [(stat_ref[mine, r, 0:1], stat_ref[mine, r, 1:2], o_ref[mine, r])]
+            for dy in range(1, across):
+                got = y_stat.at[dz, dy - 1]
+                parts.append((got[r, 0:1], got[r, 1:2], y_o[dz, dy - 1, r]))
+            best, whole, mean = combine(parts)
+            held_o[dz, r] = mean.astype(held_o.dtype)
+            held_stat[dz, r, 0:1] = best
+            held_stat[dz, r, 1:2] = whole
+        if dz:
+            device = peer(lax.rem(z + dz, deep), y, across)
+            at = (dz - 1,)
+            pair = (
+                remote(held_o.at[dz], z_o.at[at], zo_send, zo_receive, at, device),
+                remote(held_stat.at[dz], z_stat.at[at], zs_send, zs_receive, at, device),
+            )
+            for copy in pair:
+                copy.start()
+            along_z.append(pair)
+    trees = [
+        tree_part(head_rows(q_ref[r]), nk_ref[r], nv_ref[r], parents_ref[r])
+        for r in range(requests)
+    ]
+    for pair in along_z:
+        for copy in pair:
+            copy.wait_recv()
+    for r in range(requests):
+        parts = [trees[r], (held_stat[0, r, 0:1], held_stat[0, r, 1:2], held_o[0, r])]
+        for at in range(deep - 1):
+            parts.append((z_stat[at, r, 0:1], z_stat[at, r, 1:2], z_o[at, r]))
+        joined = combine(parts)[2].T.astype(out_ref.dtype)
+        for h in range(width // HEAD_SIZE):
+            out_ref[r, :, h * HEAD_SIZE : (h + 1) * HEAD_SIZE] = joined[
+                h * nodes : (h + 1) * nodes
+            ]
+    for dz, slots in along_y:
+        for pair in slots:
+            for copy in pair:
+                copy.wait_send()
+    for pair in along_z:
+        for copy in pair:
+            copy.wait_send()
+
+
+def join(queries, node_keys, node_values, parents, outs, stats):
+    ranks = outs.shape[0]
+    deep = 4
+    across = ranks // deep
+    block, stat = outs.shape[1:], stats.shape[1:]
+    semaphore = pltpu.SemaphoreType.DMA
+    by_y, by_z = (deep, across - 1), (deep - 1,)
+    return pl.pallas_call(
+        functools.partial(join_kernel, deep, across),
+        in_specs=[pl.BlockSpec(memory_space=pltpu.VMEM)] * 6,
+        out_specs=pl.BlockSpec(memory_space=pltpu.VMEM),
         out_shape=jax.ShapeDtypeStruct(queries.shape, jnp.bfloat16),
-        compiler_params=pltpu.CompilerParams(vmem_limit_bytes=32 << 20),
-    )(*operands)
+        scratch_shapes=[
+            pltpu.VMEM(by_y + block, jnp.bfloat16),
+            pltpu.VMEM(by_y + stat, jnp.float32),
+            pltpu.VMEM((deep,) + block, jnp.bfloat16),
+            pltpu.VMEM((deep,) + stat, jnp.float32),
+            pltpu.VMEM(by_z + block, jnp.bfloat16),
+            pltpu.VMEM(by_z + stat, jnp.float32),
+        ]
+        + [semaphore(by_y)] * 4
+        + [semaphore(by_z)] * 4,
+        compiler_params=pltpu.CompilerParams(
+            collective_id=1, has_side_effects=True, vmem_limit_bytes=40 << 20
+        ),
+    )(queries, node_keys, node_values, parents[:, None, :], outs, stats)
 
 
 def per_device(queries, stored_keys, stored_values, node_keys, node_values, parents, lengths):
     ranks = lax.axis_size("tensor")
     rank = lax.axis_index("tensor")
     extent = stored_keys.shape[1]
-    every = lax.all_gather(queries, "tensor", axis=0, tiled=False)
+    every = gather(queries, ranks)
     first = (rank * extent).astype(jnp.int32)[None]
     outs, stats = block_attention(every, stored_keys, stored_values, first, lengths)
-    every_stat = lax.all_gather(stats, "tensor", axis=0, tiled=False)
-    best = jnp.max(every_stat[:, :, :, 0], axis=0)
-    total = jnp.sum(every_stat[:, :, :, 1] * jnp.exp(every_stat[:, :, :, 0] - best), axis=0)
-    fraction = stats[:, :, 1] * jnp.exp(stats[:, :, 0] - best) / total
-    weighted = (outs.astype(jnp.float32) * fraction[:, :, None, :]).astype(jnp.bfloat16)
-    summed = lax.psum_scatter(weighted, "tensor", scatter_dimension=0, tiled=False)
-    own_stats = lax.dynamic_index_in_dim(jnp.stack([best, total], axis=2), rank, 0, keepdims=False)
     group = rank * KEY_VALUE_HEADS // ranks
     own_keys = lax.dynamic_slice_in_dim(node_keys, group * HEAD_SIZE, HEAD_SIZE, 2)
     own_values = lax.dynamic_slice_in_dim(node_values, group * HEAD_SIZE, HEAD_SIZE, 2)
-    attended = join(queries, own_keys, own_values, parents, summed, own_stats)
+    attended = join(queries, own_keys, own_values, parents, outs, stats)
     length = lax.axis_size("pipe")
     return lax.ppermute(attended, "pipe", [(i, (i + 1) % length) for i in range(length)])
 

time: 300 us -> 192 us (0.64)
  waiting for transfers between devices: 212 us -> 8.59 us
  Pallas kernels: 54.2 us -> 174 us
  between operations: 13.2 us -> 0.06 us
  other arithmetic: 9.96 us -> 0 us
    pallas_call x1 -> x2, Pallas kernels: 2.95 us -> 125 us  [the longest x1 65.7 us: join(): pl.pallas_call(functools.partial(join_kernel, deep, across), in_specs=[pl...]
    all_gather x2 -> x0, waiting for transfers between devices: 117 us -> none  [the longest x1 78.3 us: per_device(): every = lax.all_gather(queries, 'tensor', axis=0, tiled=False)]
    reduce_scatter x1 -> x0, waiting for transfers between devices: 85.8 us -> none  [per_device(): lax.psum_scatter(weighted, 'tensor', scatter_dimension=0, tiled=False)]
    convert_element_type x1 -> x0, other arithmetic: 5.43 us -> none  [per_device(): (outs.astype(jnp.float32) * fraction[:, :, None, :]).astype(jnp.bfloat16)]
    unnamed x16 -> x15, local copies, waits for them, and re-layouts: 8.86 us -> 8.17 us
  transfers between devices with their start and end apart: 4 -> 1, of which waited for: 4 -> 1; matrix products, arithmetic and copies ran while one was open for 0% -> 0% of each run, Pallas kernels for 0% -> 0%
where the time goes in v2:
time: 192 us
  Pallas kernels  174 us (91%)
  local copies, waits for them, and re-layouts  8.96 us (5%)
  waiting for transfers between devices  8.59 us (4%)
    pallas_call x1, Pallas kernels, join(): pl.pallas_call(functools.partial(join_kernel, deep, across), in_specs=[pl...  65.7 us
    pallas_call x1, Pallas kernels, gather(): pl.pallas_call(functools.partial(gather_kernel, deep, across), in_specs=[...  59.3 us
    pallas_call x1, Pallas kernels, block_attention(): pl.pallas_call(block_kernel, grid=(requests, KEY_VALUE_HEADS), in_specs=[...  49.2 us
    ppermute x1, waiting for transfers between devices, per_device(): lax.ppermute(attended, 'pipe', [(i, (i + 1) % length) for i in range(leng...  8.59 us
    unnamed x15, local copies, waits for them, and re-layouts  8.17 us
  transfers between devices with their start and end apart: 1, of which 1 were waited for; matrix products, arithmetic and copies ran while one was open for 0% of the time, Pallas kernels for 0%

profile of v2, /device:TPU:0, one launch (start us, length us, event | category | flops | bytes accessed | tf_op | source)
XLA Modules:
  0.0 191.8 jit_solution(11663455861330225259)
XLA Ops:
  0.0 0.0 copy-start.6
  0.0 0.0 copy-start.3
  0.0 1.1 copy-done.3
  1.1 59.3 %shard_map.73.q_ref = bf16[8,2,64,2048]{3,2,1,0:T(8,128)(2,1)S(1)} custom-call(bf16[2,64,2048]{2,1,0:T(8,128)(2,1)S(1)} %copy-done.3), custom_call_target="tpu_custom_call" | custom-call | tf_op jit(solution)/shard_map/pallas_call | solution.py:191
  60.4 0.0 copy-start
  60.4 1.9 %copy-done = bf16[8,2,64,2048]{3,2,1,0:T(8,128)(2,1)} copy-done((bf16[8,2,64,2048]{3,2,1,0:T(8,128)(2,1)}, bf16[8,2,64,2048]{3,2,1,0:T(8,128)(2,1)S(1)}, u32[]{:S(2)}) %copy-start) | copy-done | bytes 4194328
  62.3 0.8 constant_dynamic-slice_fusion
  63.1 0.0 copy-done.6
  63.1 0.0 copy-start.1
  63.1 2.2 %copy-done.1 = bf16[8,2,64,2048]{3,2,1,0:T(8,128)(2,1)S(1)} copy-done((bf16[8,2,64,2048]{3,2,1,0:T(8,128)(2,1)S(1)}, bf16[8,2,64,2048]{3,2,1,0:T(8,128)(2,1)}, u32[]{:S(2)}) %copy-start.1) | copy-done | bytes 4194328
  65.3 0.0 copy-start.2
  65.3 2.2 %copy-done.2 = bf16[2,1024,1024]{2,1,0:T(8,128)(2,1)S(1)} copy-done((bf16[2,1024,1024]{2,1,0:T(8,128)(2,1)S(1)}, bf16[2,1024,1024]{2,1,0:T(8,128)(2,1)}, u32[]{:S(2)}) %copy-start.2) | copy-done | bytes 4194328
  67.5 0.0 copy-start.4
  67.5 0.0 copy-start.5
  67.5 49.2 %shard_map.74 = (bf16[8,2,128,1024]{3,2,1,0:T(8,128)(2,1)S(1)}, f32[8,2,2,1024]{3,2,1,0:T(2,128)S(1)}) custom-call(s32[1]{0:T(128)} %bitcast.2.first_ref, s32[2]{0:T(128)S(1)} %copy-done.6, bf16[8,2,64,2048]{3,2,1,0:T(8,128)(2,1)S(1)} %copy-done.1, bf16[2,1024,1024]{2,1,0:T(8,128)(2,1)S(1)} %copy-done.2, bf16[2,1024,1024]{2,1,0:T(8,128)(2,1)} %v_ref.1), custom_call_target="tpu_custom_call" | custom-call | tf_op jit(solution)/shard_map/pallas_call | solution.py:56
  116.7 0.0 copy-done.4
  116.7 0.0 copy-done.5
  116.7 65.7 %shard_map.75 = bf16[2,64,2048]{2,1,0:T(8,128)(2,1)S(1)} custom-call(bf16[2,64,2048]{2,1,0:T(8,128)(2,1)S(1)} %copy-done.4, bf16[2,64,128]{2,1,0:T(8,128)(2,1)S(1)} %get-tuple-element.10.nk_ref, bf16[2,64,128]{2,1,0:T(8,128)(2,1)S(1)} %get-tuple-element.9.nv_ref, s32[2,1,64]{2,1,0:T(1,128)S(1)} %bitcast.4, ...), custom_call_target="tpu_custom_call" | custom-call | tf_op jit(solution)/shard_map/pallas_call | solution.py:300
  182.4 0.1 collective-permute-start
  182.4 8.6 %collective-permute-done = bf16[2,64,2048]{2,1,0:T(8,128)(2,1)S(1)} collective-permute-done((bf16[2,64,2048]{2,1,0:T(8,128)(2,1)S(1)}, bf16[2,64,2048]{2,1,0:T(8,128)(2,1)S(1)}, u32[]{:S(2)}, u32[]{:S(2)}) %collective-permute-start) | collective-permute-done | bytes 524320 | tf_op jit(solution)/shard_map/ppermute | solution.py:333
  191.0 0.8 copy.10
Async XLA Ops:
  0.0 63.1 %copy-start.6 = (s32[2]{0:T(128)S(1)}, s32[2]{0:T(128)}, u32[]{:S(2)}) copy-start(s32[2]{0:T(128)} %lengths_ref.1) | copy-start | bytes 28
  0.0 1.1 copy-start.3
  60.4 1.9 %copy-start = (bf16[8,2,64,2048]{3,2,1,0:T(8,128)(2,1)}, bf16[8,2,64,2048]{3,2,1,0:T(8,128)(2,1)S(1)}, u32[]{:S(2)}) copy-start(bf16[8,2,64,2048]{3,2,1,0:T(8,128)(2,1)S(1)} %shard_map.73.q_ref) | copy-start | bytes 12582916
  63.1 2.2 %copy-start.1 = (bf16[8,2,64,2048]{3,2,1,0:T(8,128)(2,1)S(1)}, bf16[8,2,64,2048]{3,2,1,0:T(8,128)(2,1)}, u32[]{:S(2)}) copy-start(bf16[8,2,64,2048]{3,2,1,0:T(8,128)(2,1)} %copy-done) | copy-start | bytes 12582916
  65.3 2.2 %copy-start.2 = (bf16[2,1024,1024]{2,1,0:T(8,128)(2,1)S(1)}, bf16[2,1024,1024]{2,1,0:T(8,128)(2,1)}, u32[]{:S(2)}) copy-start(bf16[2,1024,1024]{2,1,0:T(8,128)(2,1)} %k_ref.1) | copy-start | bytes 12582916
  67.5 49.2 %copy-start.4 = (bf16[2,64,2048]{2,1,0:T(8,128)(2,1)S(1)}, bf16[2,64,2048]{2,1,0:T(8,128)(2,1)}, u32[]{:S(2)}) copy-start(bf16[2,64,2048]{2,1,0:T(8,128)(2,1)} %q_ref.3) | copy-start | bytes 1572868
  67.5 49.2 %copy-start.5 = (s32[2,64]{1,0:T(2,128)S(1)}, s32[2,64]{1,0:T(2,128)}, u32[]{:S(2)}) copy-start(s32[2,64]{1,0:T(2,128)} %param.12) | copy-start | bytes 1540
  182.4 8.7 %collective-permute-start = (bf16[2,64,2048]{2,1,0:T(8,128)(2,1)S(1)}, bf16[2,64,2048]{2,1,0:T(8,128)(2,1)S(1)}, u32[]{:S(2)}, u32[]{:S(2)}) collective-permute-start(bf16[2,64,2048]{2,1,0:T(8,128)(2,1)S(1)} %shard_map.75), channel_id=1, source_target_pairs={{0,8},{8,16},{16,24},{24,0},{1,9},{9,17},{17,25},{25,1},{2,10},{10... | collective-permute-start | bytes 1572872 | tf_op jit(solution)/shard_map/ppermute | solution.py:333

commit v3 on v2

--- a/solution.py
+++ b/solution.py
@@ -21,58 +21,6 @@
     return jnp.concatenate(
         [block[:, h * HEAD_SIZE : (h + 1) * HEAD_SIZE] for h in range(heads)], axis=0
     )
-
-
-def block_kernel(first_ref, lengths_ref, q_ref, k_ref, v_ref, o_ref, stat_ref):
-    live = lengths_ref[pl.program_id(0)] - first_ref[0]
-    keys = k_ref[0]
-    values = v_ref[0]
-    positions = lax.broadcasted_iota(jnp.int32, (keys.shape[0], 1), 0)
-    active = positions < live
-    scale = HEAD_SIZE**-0.5
-    for part in range(q_ref.shape[0]):
-        heads = q_ref.shape[3] // HEAD_SIZE
-        for first in range(0, heads, 4):
-            rows = head_rows(q_ref[part, 0, :, first * HEAD_SIZE : (first + 4) * HEAD_SIZE])
-            scores = lax.dot_general(keys, rows, NT, preferred_element_type=jnp.float32)
-            scores = jnp.where(active, scores, MASKED_SCORE)
-            top = jnp.max(scores, axis=0, keepdims=True)
-            weights = jnp.exp2((scores - top) * (scale * LOG2_E))
-            total = jnp.sum(weights, axis=0, keepdims=True)
-            out = lax.dot_general(
-                values, weights.astype(jnp.bfloat16), TN, preferred_element_type=jnp.float32
-            )
-            columns = slice(first * 64, (first + 4) * 64)
-            o_ref[part, 0, :, columns] = (out / total).astype(jnp.bfloat16)
-            stat_ref[part, 0, 0:1, columns] = top * scale
-            stat_ref[part, 0, 1:2, columns] = total
-
-
-def block_attention(queries, keys, values, first, lengths):
-    ranks, requests, nodes, width = queries.shape
-    extent = keys.shape[1]
-    share = ranks // KEY_VALUE_HEADS
-    rows = width // HEAD_SIZE * nodes
-    return pl.pallas_call(
-        block_kernel,
-        grid=(requests, KEY_VALUE_HEADS),
-        in_specs=[
-            pl.BlockSpec(memory_space=pltpu.SMEM),
-            pl.BlockSpec(memory_space=pltpu.SMEM),
-            pl.BlockSpec((share, 1, nodes, width), lambda r, g: (g, r, 0, 0)),
-            pl.BlockSpec((1, extent, HEAD_SIZE), lambda r, g: (r, 0, g)),
-            pl.BlockSpec((1, extent, HEAD_SIZE), lambda r, g: (r, 0, g)),
-        ],
-        out_specs=[
-            pl.BlockSpec((share, 1, HEAD_SIZE, rows), lambda r, g: (g, r, 0, 0)),
-            pl.BlockSpec((share, 1, 2, rows), lambda r, g: (g, r, 0, 0)),
-        ],
-        out_shape=[
-            jax.ShapeDtypeStruct((ranks, requests, HEAD_SIZE, rows), jnp.bfloat16),
-            jax.ShapeDtypeStruct((ranks, requests, 2, rows), jnp.float32),
-        ],
-        compiler_params=pltpu.CompilerParams(vmem_limit_bytes=40 << 20),
-    )(first, lengths, queries, keys, values)
 
 
 def tree_part(rows, node_keys, node_values, parents):
@@ -125,85 +73,131 @@
     pl.semaphore_wait(barrier, len(partners))
 
 
-def gather_kernel(
-    deep, across, q_ref, every_ref, own_sem, z_send, z_receive, y_send, y_receive
+def block_part(live, source, keys, values, o_ref, stat_ref):
+    positions = lax.broadcasted_iota(jnp.int32, (keys.shape[0], 1), 0)
+    active = positions < live
+    scale = HEAD_SIZE**-0.5
+    nodes, width = source.shape
+    heads = 4
+    chunks = width // (heads * HEAD_SIZE)
+
+    def chunk(c):
+        across = pl.ds(pl.multiple_of(c * heads * HEAD_SIZE, heads * HEAD_SIZE), heads * HEAD_SIZE)
+        columns = pl.ds(pl.multiple_of(c * heads * nodes, heads * nodes), heads * nodes)
+        rows = head_rows(source[:, across])
+        scores = lax.dot_general(keys[...], rows, NT, preferred_element_type=jnp.float32)
+        scores = jnp.where(active, scores, MASKED_SCORE)
+        top = jnp.max(scores, axis=0, keepdims=True)
+        weights = jnp.exp2((scores - top) * (scale * LOG2_E))
+        total = jnp.sum(weights, axis=0, keepdims=True)
+        out = lax.dot_general(
+            values[...], weights.astype(jnp.bfloat16), TN, preferred_element_type=jnp.float32
+        )
+        o_ref[:, columns] = (out / total).astype(jnp.bfloat16)
+        stat_ref[0:1, columns] = top * scale
+        stat_ref[1:2, columns] = total
+
+    @pl.loop(0, chunks // 2)
+    def _(step):
+        chunk(2 * step)
+        chunk(2 * step + 1)
+
+
+def block_kernel(
+    deep, across, lengths_ref, q_ref, k_ref, v_ref, o_ref, stat_ref,
+    every_ref, z_send, z_receive, y_send, y_receive,
 ):
     rank = lax.axis_index("tensor")
     z, y = rank // across, lax.rem(rank, across)
+    share = deep * across // KEY_VALUE_HEADS
+    requests = q_ref.shape[0]
+    extent = k_ref.shape[1]
     greet(deep, across, z, y)
-    requests = q_ref.shape[0]
-    own = pltpu.make_async_copy(q_ref, every_ref.at[rank], own_sem)
-    own.start()
-    along_z, along_y = [], []
+    along_z, along_y = {}, {}
+
+    def send_y(source, slot, r, dz):
+        for dy in range(1, across):
+            at = (r, dz, dy - 1)
+            device = peer(z, lax.rem(y + dy, across), across)
+            copy = remote(source, every_ref.at[slot, r], y_send, y_receive, at, device)
+            copy.start()
+            along_y[at] = copy
+
     for r in range(requests):
         for dz in range(1, deep):
-            copy = remote(
-                q_ref.at[r],
-                every_ref.at[rank, r],
-                z_send,
-                z_receive,
-                (r, dz - 1),
-                peer(lax.rem(z + dz, deep), y, across),
-            )
+            at = (r, dz - 1)
+            device = peer(lax.rem(z + dz, deep), y, across)
+            copy = remote(q_ref.at[r], every_ref.at[rank, r], z_send, z_receive, at, device)
             copy.start()
-            along_z.append(copy)
+            along_z[at] = copy
+        send_y(q_ref.at[r], rank, r, 0)
+
+    def work(source, slot, r):
+        columns = pl.ds(pl.multiple_of(slot // share * HEAD_SIZE, HEAD_SIZE), HEAD_SIZE)
+        block_part(
+            lengths_ref[r] - rank * extent,
+            source,
+            k_ref.at[r, :, columns],
+            v_ref.at[r, :, columns],
+            o_ref.at[slot, r],
+            stat_ref.at[slot, r],
+        )
+
+    def pass_on(r, dz):
+        along_z[r, dz - 1].wait_recv()
+        slot = lax.rem(z + deep - dz, deep) * across + y
+        send_y(every_ref.at[slot, r], slot, r, dz)
+        work(every_ref.at[slot, r], slot, r)
+
+    def from_y(r, dz):
         for dy in range(1, across):
-            copy = remote(
-                q_ref.at[r],
-                every_ref.at[rank, r],
-                y_send,
-                y_receive,
-                (r, 0, dy - 1),
-                peer(z, lax.rem(y + dy, across), across),
-            )
-            copy.start()
-            along_y.append(copy)
+            along_y[r, dz, dy - 1].wait_recv()
+            other = lax.rem(y + across - dy, across)
+            slot = lax.rem(z + deep - dz, deep) * across + other
+            work(every_ref.at[slot, r], slot, r)
+
     for r in range(requests):
+        work(q_ref.at[r], rank, r)
+    for r in range(requests):
+        from_y(r, 0)
+    for dz in range(1, deep):
+        pass_on(0, dz)
+    for r in range(1, requests):
         for dz in range(1, deep):
-            source = lax.rem(z + deep - dz, deep) * across + y
-            remote(
-                q_ref.at[r], every_ref.at[source, r], z_send, z_receive, (r, dz - 1),
-                peer(lax.rem(z + dz, deep), y, across),
-            ).wait_recv()
-            for dy in range(1, across):
-                copy = remote(
-                    every_ref.at[source, r],
-                    every_ref.at[source, r],
-                    y_send,
-                    y_receive,
-                    (r, dz, dy - 1),
-                    peer(z, lax.rem(y + dy, across), across),
-                )
-                copy.start()
-                along_y.append(copy)
-    for copy in along_z:
+            pass_on(r, dz)
+            from_y(r - 1, dz)
+    for dz in range(1, deep):
+        from_y(requests - 1, dz)
+    for copy in [*along_z.values(), *along_y.values()]:
         copy.wait_send()
-    for copy in along_y:
-        copy.wait()
-    own.wait()
-
-
-def gather(queries, ranks):
+
+
+def block_attention(queries, keys, values, lengths, ranks):
+    requests, nodes, width = queries.shape
     deep = 4
     across = ranks // deep
-    requests = queries.shape[0]
+    rows = width // HEAD_SIZE * nodes
     semaphore = pltpu.SemaphoreType.DMA
+    vmem = pl.BlockSpec(memory_space=pltpu.VMEM)
     return pl.pallas_call(
-        functools.partial(gather_kernel, deep, across),
-        in_specs=[pl.BlockSpec(memory_space=pltpu.VMEM)],
-        out_specs=pl.BlockSpec(memory_space=pltpu.VMEM),
-        out_shape=jax.ShapeDtypeStruct((ranks,) + queries.shape, queries.dtype),
+        functools.partial(block_kernel, deep, across),
+        in_specs=[pl.BlockSpec(memory_space=pltpu.SMEM), vmem, vmem, vmem],
+        out_specs=[vmem, vmem],
+        out_shape=[
+            jax.ShapeDtypeStruct((ranks, requests, HEAD_SIZE, rows), jnp.bfloat16),
+            jax.ShapeDtypeStruct((ranks, requests, 2, rows), jnp.float32),
+        ],
         scratch_shapes=[
-            semaphore,
+            pltpu.VMEM((ranks,) + queries.shape, queries.dtype),
             semaphore((requests, deep - 1)),
             semaphore((requests, deep - 1)),
             semaphore((requests, deep, across - 1)),
             semaphore((requests, deep, across - 1)),
         ],
         compiler_params=pltpu.CompilerParams(
-            collective_id=0, has_side_effects=True, vmem_limit_bytes=32 << 20
+            collective_id=0, has_side_effects=True, vmem_limit_bytes=48 << 20
         ),
-    )(queries)
+    )(lengths, queries, keys, values)
 
 
 def combine(parts):
@@ -321,10 +315,7 @@
 def per_device(queries, stored_keys, stored_values, node_keys, node_values, parents, lengths):
     ranks = lax.axis_size("tensor")
     rank = lax.axis_index("tensor")
-    extent = stored_keys.shape[1]
-    every = gather(queries, ranks)
-    first = (rank * extent).astype(jnp.int32)[None]
-    outs, stats = block_attention(every, stored_keys, stored_values, first, lengths)
+    outs, stats = block_attention(queries, stored_keys, stored_values, lengths, ranks)
     group = rank * KEY_VALUE_HEADS // ranks
     own_keys = lax.dynamic_slice_in_dim(node_keys, group * HEAD_SIZE, HEAD_SIZE, 2)
     own_values = lax.dynamic_slice_in_dim(node_values, group * HEAD_SIZE, HEAD_SIZE, 2)

time: 192 us -> 151 us (0.79); the launches traced: 192 us -> 149 us
  Pallas kernels: 174 us -> 137 us
  local copies, waits for them, and re-layouts: 8.96 us -> 3.27 us
    pallas_call x2 -> x1, Pallas kernels: 108 us -> 74.5 us  [block_attention(): pl.pallas_call(functools.partial(block_kernel, deep, across), in_specs=[p...]
    unnamed x15 -> x7, local copies, waits for them, and re-layouts: 8.17 us -> 2.49 us
    pallas_call x1, Pallas kernels: 65.7 us -> 62.4 us  [join(): pl.pallas_call(functools.partial(join_kernel, deep, across), in_specs=[pl...]
where the time goes in v3:
time: 151 us; the launch traced here: 149 us
  Pallas kernels  137 us (91%)
  waiting for transfers between devices  8.59 us (6%)
  local copies, waits for them, and re-layouts  3.27 us (2%)
    pallas_call x1, Pallas kernels, block_attention(): pl.pallas_call(functools.partial(block_kernel, deep, across), in_specs=[p...  74.5 us
    pallas_call x1, Pallas kernels, join(): pl.pallas_call(functools.partial(join_kernel, deep, across), in_specs=[pl...  62.4 us
    ppermute x1, waiting for transfers between devices, per_device(): lax.ppermute(attended, 'pipe', [(i, (i + 1) % length) for i in range(leng...  8.59 us
  transfers between devices with their start and end apart: 1, of which 1 were waited for; matrix products, arithmetic and copies ran while one was open for 0% of the time, Pallas kernels for 0%

profile of v3, /device:TPU:0, one launch (start us, length us, event | category | flops | bytes accessed | tf_op | source)
XLA Modules:
  0.0 148.8 jit_solution(11551034938884361052)
XLA Ops:
  0.0 0.8 constant_dynamic-slice_fusion
  0.8 0.0 copy-start
  0.8 1.0 copy-done
  1.8 0.0 copy-start.2
  1.8 0.7 copy-done.2
  2.5 0.0 copy-start.1
  2.5 74.5 %shard_map.73 = (bf16[8,2,128,1024]{3,2,1,0:T(8,128)(2,1)S(1)}, f32[8,2,2,1024]{3,2,1,0:T(2,128)S(1)}) custom-call(s32[2]{0:T(128)S(1)} %copy-done.2, bf16[2,64,2048]{2,1,0:T(8,128)(2,1)S(1)} %copy-done, bf16[2,1024,1024]{2,1,0:T(8,128)(2,1)} %k_ref.1, bf16[2,1024,1024]{2,1,0:T(8,128)(2,1)} %v_ref.1), custom_call_target="tpu_custom_call" | custom-call | tf_op jit(solution)/shard_map/pallas_call | solution.py:182
  76.9 0.0 copy-done.1
  77.0 62.4 %shard_map.74 = bf16[2,64,2048]{2,1,0:T(8,128)(2,1)S(1)} custom-call(bf16[2,64,2048]{2,1,0:T(8,128)(2,1)S(1)} %copy-done, bf16[2,64,128]{2,1,0:T(8,128)(2,1)S(1)} %get-tuple-element.10.nk_ref, bf16[2,64,128]{2,1,0:T(8,128)(2,1)S(1)} %get-tuple-element.9.nv_ref, s32[2,1,64]{2,1,0:T(1,128)S(1)} %bitcast.3, ...), custom_call_target="tpu_custom_call" | custom-call | tf_op jit(solution)/shard_map/pallas_call | solution.py:294
  139.3 0.1 collective-permute-start
  139.4 8.6 %collective-permute-done = bf16[2,64,2048]{2,1,0:T(8,128)(2,1)S(1)} collective-permute-done((bf16[2,64,2048]{2,1,0:T(8,128)(2,1)S(1)}, bf16[2,64,2048]{2,1,0:T(8,128)(2,1)S(1)}, u32[]{:S(2)}, u32[]{:S(2)}) %collective-permute-start) | collective-permute-done | bytes 524320 | tf_op jit(solution)/shard_map/ppermute | solution.py:324
  148.0 0.8 copy.10
Async XLA Ops:
  0.8 1.0 copy-start
  1.8 0.7 copy-start.2
  2.5 74.5 %copy-start.1 = (s32[2,64]{1,0:T(2,128)S(1)}, s32[2,64]{1,0:T(2,128)}, u32[]{:S(2)}) copy-start(s32[2,64]{1,0:T(2,128)} %param.12) | copy-start | bytes 1540
  139.3 8.7 %collective-permute-start = (bf16[2,64,2048]{2,1,0:T(8,128)(2,1)S(1)}, bf16[2,64,2048]{2,1,0:T(8,128)(2,1)S(1)}, u32[]{:S(2)}, u32[]{:S(2)}) collective-permute-start(bf16[2,64,2048]{2,1,0:T(8,128)(2,1)S(1)} %shard_map.74), channel_id=1, source_target_pairs={{0,8},{8,16},{16,24},{24,0},{1,9},{9,17},{17,25},{25,1},{2,10},{10... | collective-permute-start | bytes 1572872 | tf_op jit(solution)/shard_map/ppermute | solution.py:324
